TPU v7x, 32 devices: a whole 2x2x4 slice. The times are simulated.
32 devices in a mesh: sub: 8 (over z, x), blk: 4 (over y, core).
Axes of the slice: x: 2, y: 2, z: 4, core: 2. Of those that a mesh axis runs over, the one named last changes fastest.
Arguments:
- factor: bfloat16 [16, 2048, 2048], P('sub', None, 'blk'), may hold values from -0.125 to 0.125
- samples: bfloat16 [16, 2048, 128], P('sub', 'blk'), may hold values from -6 to 6
- diagonal: bfloat16 [16, 128, 16], P('sub'), may hold values from 0.25 to 1
- coupling: bfloat16 [16, 64, 2048], P('sub', 'blk'), may hold values from -0.125 to 0.125
- blocks: int32 [16], P('sub'), may hold values from 80 to 128, as said below
- peer_device: int32 [16, 128], P('sub'), may hold values from 0 to 7, as said below
- peer_lane: int32 [16, 128], P('sub'), may hold values from 0 to 34, as said below
- owns_face: int32 [16, 128], P('sub'), may hold values from 0 to 1, as said below
Outputs:
- interior: bfloat16 [16, 64, 128], P('sub', 'blk')
Inputs may be any that keep to these rules, and one draw needn't show every extreme that they name: Each subdomain's interface has blocks face blocks; over the subdomains of one index of sub they sum to 208. `peer_device`: live slots are matched in pairs of partners as the statement says, one owning side each; each index of sub owns 104 faces and holds 104 faces owned elsewhere; all faces between two indices of sub are owned by the same one of them; slots that are not live hold 0. Live slots of one index of sub with the same peer_device and the same owns_face have different peer_lane; slots that are not live hold 0. `owns_face`: slots that are not live hold 0.
All inputs are finite; a program needn't handle non-finite values.
Results may differ from a plain program's by a relative error of at most 0.013.
Values may be sent and summed in bfloat16 or wider, within the bound.
A program may use at most 64 MiB of HBM per device.

v0:
```python
import jax
import jax.numpy as jnp
from jax import lax
from jax.sharding import PartitionSpec as P

FACE_HALF = 104


def local(factor, samples, diagonal, coupling, blocks, peer_device, peer_lane, owns_face):
    sub_count = lax.axis_size("sub")
    blk_count = lax.axis_size("blk")
    blk_here = lax.axis_index("blk")
    local_subs, order, quarter = factor.shape
    slot_count, tile_rows = (diagonal.shape[1], diagonal.shape[2])
    columns = samples.shape[2]
    part_cols = columns // blk_count
    live_rows = blocks * tile_rows
    sample_rows = blk_here * quarter + jnp.arange(quarter, dtype=jnp.int32)
    row_alive = sample_rows[None, :, None] < live_rows[:, None, None]
    driven = jnp.where(row_alive, samples, jnp.zeros_like(samples))
    reduced_sum = jnp.einsum(
        "srq,src->sqc",
        factor,
        lax.all_gather(driven, "blk", axis=1, tiled=True),
        preferred_element_type=jnp.float32,
    )
    reduced = jnp.where(row_alive, reduced_sum, jnp.zeros_like(reduced_sum)).astype(jnp.bfloat16)
    summed = lax.psum_scatter(
        jnp.einsum("sqc,soq->cso", reduced, factor, preferred_element_type=jnp.float32).astype(
            jnp.bfloat16
        ),
        "blk",
        scatter_dimension=0,
        tiled=True,
    )
    slots = local_subs * slot_count
    slot_traces = (
        summed.reshape(part_cols, slots, tile_rows)
        .transpose(1, 0, 2)
        .reshape(slots, part_cols * tile_rows)
    )
    slot_diag = diagonal.reshape(slots, tile_rows)
    position = jnp.arange(slots, dtype=jnp.int32) % slot_count
    live_slot = position < jnp.repeat(blocks, slot_count)
    half_cycle = (sub_count - 1) // 2
    capacity = (FACE_HALF + half_cycle - 1) // half_cycle
    target_slot = peer_device.reshape(-1) * capacity + peer_lane.reshape(-1)
    buffer_slots = jnp.arange(sub_count * capacity, dtype=jnp.int32)

    def place(picker, values):
        placed = jnp.dot(picker, values, preferred_element_type=jnp.float32).astype(jnp.bfloat16)
        return placed.reshape(sub_count, capacity, values.shape[1])

    def collect(picker, received):
        flattened = received.reshape(sub_count * capacity, received.shape[2])
        return jnp.einsum("tx,ty->xy", picker, flattened, preferred_element_type=jnp.float32)

    every_pick = ((buffer_slots[:, None] == target_slot[None, :]) & live_slot[None, :]).astype(
        jnp.bfloat16
    )
    got_traces, got_diag = (
        lax.all_to_all(
            place(every_pick, slot_traces), "sub", split_axis=0, concat_axis=0, tiled=True
        ),
        lax.all_to_all(
            place(every_pick, slot_diag), "sub", split_axis=0, concat_axis=0, tiled=True
        ),
    )
    running = slot_traces.astype(jnp.float32).reshape(slots, part_cols, tile_rows) + collect(
        every_pick, got_traces
    ).reshape(slots, part_cols, tile_rows)
    divisor = slot_diag.astype(jnp.float32) + collect(every_pick, got_diag)
    assembled = (
        (running / divisor[:, None, :]).astype(jnp.bfloat16).reshape(slots, part_cols * tile_rows)
    )
    coefs = jnp.where(live_slot[:, None], assembled, jnp.zeros_like(assembled))
    coef_blocks = coefs.reshape(local_subs, slot_count, part_cols, tile_rows)
    inner_rows = coupling.shape[1]
    coupling_blocks = coupling.reshape(local_subs, inner_rows, slot_count, tile_rows)
    return jnp.einsum(
        "srjt,sjct->src",
        coupling_blocks,
        lax.all_gather(coef_blocks, "blk", axis=2, tiled=True),
        preferred_element_type=jnp.float32,
    ).astype(jnp.bfloat16)


def solution(mesh):
    placed = (
        P("sub", None, "blk"),
        P("sub", "blk", None),
        P("sub", None, None),
        P("sub", "blk", None),
        P("sub"),
        P("sub", None),
        P("sub", None),
        P("sub", None),
    )
    return jax.shard_map(
        local, mesh=mesh, in_specs=placed, out_specs=P("sub", "blk", None), check_vma=False
    )
```

profile of v0, /device:TPU:0, one launch (start us, length us, event | category | flops | bytes accessed | tf_op | source)
XLA Modules:
  0.0 105.2 jit_solution(14190838189797214555)
XLA Ops:
  6.5 0.7 broadcast_multiply_fusion
  7.2 1.1 %copy.29 = bf16[2,512,128]{1,2,0:T(8,128)(2,1)S(1)} copy(bf16[2,512,128]{2,1,0:T(8,128)(2,1)} %param.9) | data formatting | bytes 524288 | tf_op args[1]
  8.3 0.1 broadcast_compare_fusion
  8.4 0.7 broadcast_select_fusion
  9.2 0.0 reduce-scatter.2.cloned.1.call-start
  9.2 19.5 %all-gather.3.cloned.1.call-done = bf16[2,2048,128]{1,2,0:T(8,128)(2,1)} async-done(((bf16[2,512,128]{1,2,0:T(8,128)(2,1)}), bf16[2,2048,128]{1,2,0:T(8,128)(2,1)}) %all-gather.3.cloned.1.call-update) | async-done | bytes 1048592 | tf_op jit(solution)/shard_map/all_gather | solution.py:24
  28.7 6.8 %fusion = bf16[128,2,2048]{2,0,1:T(8,128)(2,1)} fusion(bf16[2,2048,512]{2,1,0:T(8,128)(2,1)} %param.8, bf16[2,2048,128]{1,2,0:T(8,128)(2,1)} %all-gather.3.cloned.1.call-done, pred[2,512]{1,0:T(4,128)(4,1)S(1)} %broadcast_compare_fusion), kind=kOutput, calls=%fused_computation.1 | convolution fusion | flops 1074528256 | bytes 6292480 | tf_op jit(solution)/shard_map/sqc,soq->cso/dot_general | solution.py:29
  35.6 0.1 fusion.26
  35.7 0.2 convolution_convert_fusion.2
  35.8 0.1 reshape.126
  36.0 0.7 reshape.132
  36.7 5.5 %all-to-all-start.1 = ((bf16[8,2,280]{2,1,0:T(2,128)(2,1)}), bf16[8,2,280]{2,1,0:T(2,128)(2,1)S(1)}, u32[]{:S(2)}, u32[]{:S(2)}) async-start(bf16[8,2,280]{2,1,0:T(2,128)(2,1)} %reshape.132), calls=%async_computation.2 | async-start | bytes 24576 | tf_op jit(solution)/shard_map/all_to_all | solution.py:65
  42.2 18.4 %reduce-scatter.2.cloned.1.call-done = bf16[32,2,2048]{2,0,1:T(8,128)(2,1)} async-done(((bf16[128,2,2048]{2,0,1:T(8,128)(2,1)}), bf16[32,2,2048]{2,0,1:T(8,128)(2,1)}) %reduce-scatter.2.cloned.1.call-update) | async-done | bytes 262160 | tf_op jit(solution)/shard_map/reduce_scatter | solution.py:28
  60.6 1.4 %copy.30 = bf16[32,2,2048]{0,2,1:T(8,128)(2,1)S(1)} copy(bf16[32,2,2048]{2,0,1:T(8,128)(2,1)} %reduce-scatter.2.cloned.1.call-done) | data formatting | bytes 524288 | tf_op jit(solution)/shard_map/reduce_scatter | solution.py:28
  62.0 1.1 %copy.32 = bf16[256,32,16]{0,2,1:T(8,128)(2,1)S(1)} copy(bf16[256,32,16]{1,2,0:T(8,128)(2,1)S(1)} %bitcast.55) | data formatting | bytes 524288 | tf_op jit(solution)/shard_map/transpose | solution.py:39
  63.1 0.3 convolution_convert_fusion.1
  63.4 0.8 reshape.123
  64.2 5.5 %all-to-all-start = ((bf16[8,35,512]{2,1,0:T(8,128)(2,1)}), bf16[8,35,512]{2,1,0:T(8,128)(2,1)S(1)}, u32[]{:S(2)}, u32[]{:S(2)}) async-start(bf16[8,35,512]{2,1,0:T(8,128)(2,1)} %reshape.123), calls=%async_computation.1 | async-start | bytes 655360 | tf_op jit(solution)/shard_map/all_to_all | solution.py:62
  69.8 0.1 fusion.27
  69.9 0.1 reshape.133
  70.0 0.1 reshape.127
  70.1 0.2 convolution_add_fusion.1
  70.3 0.9 copy.31
  71.1 9.0 %all-to-all-done = bf16[8,35,512]{2,1,0:T(8,128)(2,1)S(1)} async-done(((bf16[8,35,512]{2,1,0:T(8,128)(2,1)}), bf16[8,35,512]{2,1,0:T(8,128)(2,1)S(1)}, u32[]{:S(2)}, u32[]{:S(2)}) %all-to-all-start) | async-done | bytes 286752 | tf_op jit(solution)/shard_map/all_to_all | solution.py:62
  80.1 0.1 reshape.124
  80.2 0.2 copy.33
  80.4 0.3 fusion.4
  80.7 0.7 bitcast_select_fusion
  81.5 0.8 reshape.129
  82.4 0.4 copy.39
  82.8 13.7 %all-gather.5.cloned.1.call-done = bf16[2,128,128,16]{1,2,3,0:T(8,128)(2,1)} async-done(((bf16[2,128,32,16]{1,2,3,0:T(8,128)(2,1)}), bf16[2,128,128,16]{1,2,3,0:T(8,128)(2,1)}) %all-gather.5.cloned.1.call-update) | async-done | bytes 1048592 | tf_op jit(solution)/shard_map/all_gather | solution.py:83
  96.5 2.2 %fusion.6 = bf16[2,16,128]{2,1,0:T(8,128)(2,1)} fusion(bf16[2,128,128,16]{1,2,3,0:T(8,128)(2,1)} %all-gather.5.cloned.1.call-done, bf16[2,16,128,16]{2,1,3,0:T(8,128)(2,1)S(1)} %copy.39), kind=kOutput, calls=%fused_computation.13 | convolution fusion | flops 16781312 | bytes 1187840 | tf_op jit(solution)/shard_map/srjt,sjct->src/dot_general | solution.py:80
  (20 shorter events, 0.1 us)
Async XLA Ops:
  6.5 29.1 %copy-start = (bf16[2,128,16]{1,2,0:T(8,128)(2,1)S(1)}, bf16[2,128,16]{1,2,0:T(8,128)(2,1)}, u32[]{:S(2)}) copy-start(bf16[2,128,16]{1,2,0:T(8,128)(2,1)} %param.10) | copy-start | bytes 24580
  6.5 22.2 %all-gather.3.cloned.1.call-start = ((), (), s32[]{:S(2)}) async-start(), calls=%async_computation.3 | async-start | bytes 1310720 | tf_op jit(solution)/shard_map/all_gather | solution.py:24
  9.1 26.4 %copy-start.4 = (s32[2]{0:T(128)S(1)}, s32[2]{0:T(128)}, u32[]{:S(2)}) copy-start(s32[2]{0:T(128)} %param.12) | copy-start | bytes 28
  9.1 26.5 %copy-start.2 = (s32[2,128]{1,0:T(2,128)S(1)}, s32[2,128]{1,0:T(2,128)}, u32[]{:S(2)}) copy-start(s32[2,128]{1,0:T(2,128)} %param.14) | copy-start | bytes 3076
  9.2 26.5 %copy-start.3 = (s32[2,128]{1,0:T(2,128)S(1)}, s32[2,128]{1,0:T(2,128)}, u32[]{:S(2)}) copy-start(s32[2,128]{1,0:T(2,128)} %param.13) | copy-start | bytes 3076
  9.2 51.4 %reduce-scatter.2.cloned.1.call-start = ((), (), s32[]{:S(2)}) async-start(), calls=%async_computation.4 | async-start | bytes 1310720 | tf_op jit(solution)/shard_map/reduce_scatter | solution.py:28
  36.7 27.6 %all-to-all-start.1 = ((bf16[8,2,280]{2,1,0:T(2,128)(2,1)}), bf16[8,2,280]{2,1,0:T(2,128)(2,1)S(1)}, u32[]{:S(2)}, u32[]{:S(2)}) async-start(bf16[8,2,280]{2,1,0:T(2,128)(2,1)} %reshape.132), calls=%async_computation.2 | async-start | bytes 24576 | tf_op jit(solution)/shard_map/all_to_all | solution.py:65
  63.1 18.4 %copy-start.1 = (bf16[2,16,2048]{2,1,0:T(8,128)(2,1)S(1)}, bf16[2,16,2048]{2,1,0:T(8,128)(2,1)}, u32[]{:S(2)}) copy-start(bf16[2,16,2048]{2,1,0:T(8,128)(2,1)} %param.11) | copy-start | bytes 393220
  64.2 15.8 %all-to-all-start = ((bf16[8,35,512]{2,1,0:T(8,128)(2,1)}), bf16[8,35,512]{2,1,0:T(8,128)(2,1)S(1)}, u32[]{:S(2)}, u32[]{:S(2)}) async-start(bf16[8,35,512]{2,1,0:T(8,128)(2,1)} %reshape.123), calls=%async_computation.1 | async-start | bytes 655360 | tf_op jit(solution)/shard_map/all_to_all | solution.py:62
  69.8 26.7 %all-gather.5.cloned.1.call-start = ((), (), s32[]{:S(2)}) async-start(), calls=%async_computation.5 | async-start | bytes 1310720 | tf_op jit(solution)/shard_map/all_gather | solution.py:83
Sparse Core Ops, SparseCore 0:
  9.2 19.4 all-gather.2
  35.7 24.8 reduce-scatter.1
  81.6 14.7 all-gather.4
where the time goes:
time: 106 us; the launch traced here: 105 us
  waiting for transfers between devices  60.6 us (57%)
  between operations  13.3 us (13%)
  starting transfers between devices  11.1 us (10%)
  matrix products  9.99 us (9%)
  local copies, waits for them, and re-layouts  7.84 us (7%)
  other arithmetic  2.36 us (2%)
    all_gather x1, waiting for transfers between devices, local(): lax.all_gather(driven, 'blk', axis=1, tiled=True)  19.5 us
    reduce_scatter x1, waiting for transfers between devices, local(): lax.psum_scatter(jnp.einsum('sqc,soq->cso', reduced, factor, preferred_el...  18.4 us
    all_gather x1, waiting for transfers between devices, local(): lax.all_gather(coef_blocks, 'blk', axis=2, tiled=True)  13.7 us
    all_to_all x1, waiting for transfers between devices, local(): lax.all_to_all(place(every_pick, slot_traces), 'sub', split_axis=0, conca...  8.96 us
    dot_general x1, matrix products, local(): jnp.einsum('sqc,soq->cso', reduced, factor, preferred_element_type=jnp.fl...  6.82 us
    all_to_all x1, starting transfers between devices, local(): lax.all_to_all(place(every_pick, slot_traces), 'sub', split_axis=0, conca...  5.52 us
    all_to_all x1, starting transfers between devices, local(): lax.all_to_all(place(every_pick, slot_diag), 'sub', split_axis=0, concat_...  5.52 us
    dot_general x1, matrix products, local(): jnp.einsum('srjt,sjct->src', coupling_blocks, lax.all_gather(coef_blocks,...  2.21 us
  transfers between devices with their start and end apart: 5, of which 4 were waited for; matrix products, arithmetic and copies ran while one was open for 7% of the time, Pallas kernels for 0%

commit v1 on v0

v1 whole, which is shorter than its diff:
```python
import functools

import jax
import jax.numpy as jnp
from jax import lax
from jax.experimental import pallas as pl
from jax.experimental.pallas import tpu as pltpu
from jax.sharding import PartitionSpec as P

FACE_HALF = 104
MESH = pl.DeviceIdType.MESH
F32, BF16 = jnp.float32, jnp.bfloat16


def kernel(
    n_sub, n_blk, pad,
    factor, samples, diagonal, coupling, blocks, peer_device, peer_lane, out,
    fac, drv, tr, parts, near, far, mixed, kept, place, face_out, face_in,
    coup_t, coup_out, coup_in, inner, inner_in, diag_pad,
    local_sem, near_sem, far_sem, relay_sem, near_sum, far_sum, face_sem, coup_sem, last_sem,
):
    me, here = lax.axis_index("sub"), lax.axis_index("blk")
    subs, order, quarter = fac.shape
    slots_one, tile = diagonal.shape[1], diagonal.shape[2]
    slots = subs * slots_one
    cols = samples.shape[2]
    mine = tile // n_blk
    inner_rows = coupling.shape[1]
    twin = here + 1 - 2 * lax.rem(here, 2)
    cross = lax.rem(here + 2, n_blk)
    diag = lax.rem(twin + 2, n_blk)

    def remote(src, dst, sems, where):
        return pltpu.make_async_remote_copy(
            src_ref=src, dst_ref=dst, send_sem=sems.at[0], recv_sem=sems.at[1],
            device_id=where, device_id_type=MESH,
        )

    def sub_peer(step):
        return lax.rem(me + step, n_sub)

    load = []
    for s in range(subs):
        one = pltpu.make_async_copy(factor.at[s], fac.at[s], local_sem.at[s])
        one.start()
        load.append(one)
    own = pltpu.make_async_copy(samples, drv.at[here], local_sem.at[subs])
    own.start()

    barrier = pltpu.get_barrier_semaphore()
    for b in (twin, cross, diag):
        pl.semaphore_signal(barrier, inc=1, device_id={"blk": b}, device_id_type=MESH)

    def greet(step, carry):
        pl.semaphore_signal(
            barrier, inc=1, device_id={"sub": sub_peer(step)}, device_id_type=MESH
        )
        return carry

    lax.fori_loop(1, n_sub, greet, 0)
    pl.semaphore_wait(barrier, n_sub - 1 + 3)

    to_far = [
        remote(samples.at[s], drv.at[here, s], far_sem.at[s], {"blk": cross}) for s in range(subs)
    ]
    to_near = [
        remote(samples.at[s], drv.at[here, s], near_sem.at[s], {"blk": twin}) for s in range(subs)
    ]
    for s in range(subs):
        to_far[s].start()
    for s in range(subs):
        to_near[s].start()

    rows = n_sub * pad
    slot_of = lax.broadcasted_iota(jnp.int32, (1, slots_one), 1)
    columns = []
    for s in range(subs):
        row = peer_device[pl.ds(s, 1), :] * pad + peer_lane[pl.ds(s, 1), :]
        row = jnp.where(slot_of < blocks[s], row, -1)
        row_of = lax.broadcasted_iota(jnp.int32, (rows, slots_one), 0)
        place[:, s * slots_one:(s + 1) * slots_one] = jnp.where(row_of == row, 1.0, 0.0).astype(BF16)
        columns.append(jnp.broadcast_to(row.astype(F32), (slots_one, slots_one)).T[:, :1])
    column = jnp.concatenate(columns, axis=0).astype(jnp.int32)
    live = column >= 0
    inside = (column >= me * pad) & (column < me * pad + pad)
    lane_of = lax.broadcasted_iota(jnp.int32, (slots, rows), 1)
    collect = jnp.where(lane_of == column, 1.0, 0.0).astype(BF16)
    self_rows = pl.ds(pl.multiple_of(me * pad, 16), pad)

    def face_copy(k, step):
        there = pl.ds(pl.multiple_of(sub_peer(step) * pad, 16), pad)
        return remote(
            face_out.at[k, there], face_in.at[k, self_rows], face_sem.at[k], {"sub": sub_peer(step)}
        )

    def send_faces(k, value):
        face_out[k] = jnp.dot(place[...], value, preferred_element_type=F32).astype(BF16)
        face_in[k, self_rows, :] = face_out[k, self_rows, :]

        def go(step, carry):
            face_copy(k, step).start()
            return carry

        lax.fori_loop(1, n_sub, go, 0)

    def faces(k, value):
        all_rows = pl.ds(0, (n_sub - 1) * pad)
        remote(
            face_out.at[k, all_rows], face_in.at[k, all_rows], face_sem.at[k], {"sub": sub_peer(1)}
        ).wait()
        got = jnp.dot(collect, face_in[k], preferred_element_type=F32)
        return jnp.where(inside, 0.0, value.astype(F32)) + got

    diag_pad[...] = jnp.zeros_like(diag_pad)
    diag_pad[:, :tile] = diagonal[...].reshape(slots, tile)
    send_faces(mine, diag_pad[...])

    wide = coupling[...].reshape(subs * inner_rows, order).astype(F32)
    filler = jnp.zeros((coup_t.shape[1] - subs * inner_rows, order), F32)
    coup_t[...] = jnp.concatenate([wide, filler], axis=0).T
    for t in range(tile):
        piece = coup_t[pl.ds(t, slots_one, stride=tile), :].T
        coup_out[t] = piece[:subs * inner_rows].astype(BF16)
    coup_in[here] = coup_out[pl.ds(here * mine, mine)]
    coup_copies = [
        remote(coup_out.at[pl.ds(b * mine, mine)], coup_in.at[here], coup_sem.at[i], {"blk": b})
        for i, b in enumerate((twin, cross, diag))
    ]
    for c in coup_copies:
        c.start()

    own.wait()
    relays = []
    row_in = lax.broadcasted_iota(jnp.int32, (quarter, 1), 0)
    lane_in = lax.broadcasted_iota(jnp.int32, (1, quarter), 1)

    def first(s, b):
        begin = pl.multiple_of(b * quarter, quarter)
        rows_live = row_in + begin < blocks[s] * tile
        value = drv[b, s]
        value = jnp.where(rows_live, value, jnp.zeros_like(value))
        return lax.dot_general(
            value, fac[s, pl.ds(begin, quarter), :], (((0,), (0,)), ((), ())),
            preferred_element_type=F32,
        )

    for s in range(subs):
        load[s].wait()
        reduced = first(s, here)
        to_near[s].wait()
        reduced += first(s, twin)
        to_far[s].wait()
        relay = remote(drv.at[cross, s], drv.at[cross, s], relay_sem.at[s], {"blk": twin})
        relay.start()
        reduced += first(s, cross)
        relay.wait()
        reduced += first(s, diag)
        alive = lane_in + here * quarter < blocks[s] * tile
        reduced = jnp.where(alive, reduced, 0.0).astype(BF16)
        for q in range(0, order, quarter):
            tr[s, q:q + quarter, :] = lax.dot_general(
                fac[s, q:q + quarter, :], reduced, (((1,), (1,)), ((), ())),
                preferred_element_type=F32,
            )
        for t in range(tile):
            parts[t, s * slots_one:(s + 1) * slots_one, :] = tr[
                s, pl.ds(t, slots_one, stride=tile), :
            ].astype(BF16)

    near_copies = []
    for k in range(mine):
        pair = [
            remote(parts.at[diag * mine + k], near.at[k, 1], near_sum.at[k, 1], {"blk": twin}),
            remote(parts.at[twin * mine + k], near.at[k, 0], near_sum.at[k, 0], {"blk": twin}),
        ]
        for c in pair:
            c.start()
        near_copies.append(pair)
    far_copies = []
    for k in range(mine):
        near_copies[k][0].wait()
        mixed[k] = (parts[cross * mine + k].astype(F32) + near[k, 1].astype(F32)).astype(BF16)
        c = remote(mixed.at[k], far.at[k], far_sum.at[k], {"blk": cross})
        c.start()
        far_copies.append(c)
    for k in range(mine):
        near_copies[k][1].wait()
        far_copies[k].wait()
        kept[k] = (
            parts[here * mine + k].astype(F32) + near[k, 0].astype(F32) + far[k].astype(F32)
        ).astype(BF16)
        send_faces(k, kept[k])

    for c in coup_copies:
        c.wait()
    divisors = faces(mine, diag_pad[...])
    lane_t = lax.broadcasted_iota(jnp.int32, (slots, cols), 1)
    sums = [None] * subs
    for k in range(mine):
        divisor = jnp.sum(
            jnp.where(lane_t == here * mine + k, divisors, 0.0), axis=1, keepdims=True
        )
        divisor = jnp.where(live, divisor, 1.0)
        coef = jnp.where(live, faces(k, kept[k]) / divisor, 0.0).astype(BF16)
        for s in range(subs):
            left = coup_in[:, k, s * inner_rows:(s + 1) * inner_rows, :]
            got = jnp.dot(
                left.reshape(n_blk * inner_rows, slots_one),
                coef[s * slots_one:(s + 1) * slots_one],
                preferred_element_type=F32,
            )
            sums[s] = got if k == 0 else sums[s] + got
    for s in range(subs):
        inner[:, s] = sums[s].reshape(n_blk, inner_rows, cols)
    last = [
        remote(inner.at[b], inner_in.at[here], last_sem.at[i], {"blk": b})
        for i, b in enumerate((twin, cross, diag))
    ]
    for c in last:
        c.start()
    total = inner[here]
    for c in last:
        c.wait()
    for b in (twin, cross, diag):
        total = total + inner_in[b]
    out[...] = total.astype(BF16)


def local(factor, samples, diagonal, coupling, blocks, peer_device, peer_lane, owns_face):
    n_sub, n_blk = lax.axis_size("sub"), lax.axis_size("blk")
    subs, order, quarter = factor.shape
    slots_one, tile = diagonal.shape[1], diagonal.shape[2]
    slots, cols = subs * slots_one, samples.shape[2]
    mine, inner_rows = tile // n_blk, coupling.shape[1]
    half_cycle = (n_sub - 1) // 2
    capacity = (FACE_HALF + half_cycle - 1) // half_cycle
    pad = -(-capacity // 16) * 16
    rows = n_sub * pad
    flops = 4 * subs * order * quarter * cols
    vmem, hbm = pl.BlockSpec(memory_space=pltpu.VMEM), pl.BlockSpec(memory_space=pl.ANY)
    smem = pl.BlockSpec(memory_space=pltpu.SMEM)
    sem = pltpu.SemaphoreType.DMA
    coup_lanes = -(-subs * inner_rows // 128) * 128
    return pl.pallas_call(
        functools.partial(kernel, n_sub, n_blk, pad),
        out_shape=jax.ShapeDtypeStruct((subs, inner_rows, cols), BF16),
        in_specs=[hbm, hbm, vmem, vmem, smem, vmem, vmem],
        out_specs=vmem,
        scratch_shapes=[
            pltpu.VMEM((subs, order, quarter), BF16),
            pltpu.VMEM((n_blk, subs, quarter, cols), BF16),
            pltpu.VMEM((subs, order, cols), F32),
            pltpu.VMEM((tile, slots, cols), BF16),
            pltpu.VMEM((mine, 2, slots, cols), BF16),
            pltpu.VMEM((mine, slots, cols), BF16),
            pltpu.VMEM((mine, slots, cols), BF16),
            pltpu.VMEM((mine, slots, cols), BF16),
            pltpu.VMEM((rows, slots), BF16),
            pltpu.VMEM((mine + 1, rows, cols), BF16),
            pltpu.VMEM((mine + 1, rows, cols), BF16),
            pltpu.VMEM((order, coup_lanes), F32),
            pltpu.VMEM((tile, subs * inner_rows, slots_one), BF16),
            pltpu.VMEM((n_blk, mine, subs * inner_rows, slots_one), BF16),
            pltpu.VMEM((n_blk, subs, inner_rows, cols), F32),
            pltpu.VMEM((n_blk, subs, inner_rows, cols), F32),
            pltpu.VMEM((slots, cols), BF16),
            sem((subs + 1,)),
            sem((subs, 2)),
            sem((subs, 2)),
            sem((subs, 2)),
            sem((mine, 2, 2)),
            sem((mine, 2)),
            sem((mine + 1, 2)),
            sem((3, 2)),
            sem((3, 2)),
        ],
        compiler_params=pltpu.CompilerParams(
            collective_id=0, has_side_effects=True, vmem_limit_bytes=48 * 1024 * 1024
        ),
        cost_estimate=pl.CostEstimate(
            flops=flops, bytes_accessed=2 * factor.size, transcendentals=0
        ),
    )(factor, samples, diagonal, coupling, blocks, peer_device, peer_lane)


def solution(mesh):
    placed = (
        P("sub", None, "blk"),
        P("sub", "blk", None),
        P("sub", None, None),
        P("sub", "blk", None),
        P("sub"),
        P("sub", None),
        P("sub", None),
        P("sub", None),
    )
    return jax.shard_map(
        local, mesh=mesh, in_specs=placed, out_specs=P("sub", "blk", None), check_vma=False
    )
```

time: 106 us -> 43.6 us (0.41)
  waiting for transfers between devices: 60.6 us -> 0 us
  Pallas kernels: 0 us -> 35.8 us
  between operations: 13.3 us -> 0.02 us
  starting transfers between devices: 11.1 us -> 0 us
  matrix products: 9.99 us -> 0 us
  other arithmetic: 2.36 us -> 0 us
    pallas_call x0 -> x1, Pallas kernels: none -> 35.8 us  [local(): pl.pallas_call(functools.partial(kernel, n_sub, n_blk, pad), out_shape=ja...]
    all_gather x2 -> x0, waiting for transfers between devices: 33.2 us -> none  [the longest x1 19.5 us: local(): lax.all_gather(driven, 'blk', axis=1, tiled=True)]
    reduce_scatter x1 -> x0, waiting for transfers between devices: 18.4 us -> none  [local(): lax.psum_scatter(jnp.einsum('sqc,soq->cso', reduced, factor, preferred_el...]
    all_to_all x2 -> x0, starting transfers between devices: 11 us -> none  [the longest x1 5.52 us: local(): lax.all_to_all(place(every_pick, slot_traces), 'sub', split_axis=0, conca...]
    dot_general x6 -> x0, matrix products: 9.99 us -> none  [the longest x1 6.82 us: local(): jnp.einsum('sqc,soq->cso', reduced, factor, preferred_element_type=jnp.fl...]
    all_to_all x2 -> x0, waiting for transfers between devices: 8.96 us -> none  [the longest x1 8.96 us: local(): lax.all_to_all(place(every_pick, slot_traces), 'sub', split_axis=0, conca...]
    unnamed x13 -> x14, local copies, waits for them, and re-layouts: 1.91 us -> 7.47 us
    reshape x8 -> x0, local copies, waits for them, and re-layouts: 3.2 us -> none  [the longest x2 1.21 us: local(): coupling.reshape(local_subs, inner_rows, slot_count, tile_rows)]
  transfers between devices with their start and end apart: 5 -> 0, of which waited for: 4 -> 0; matrix products, arithmetic and copies ran while one was open for 7% -> 0% of each run, Pallas kernels for 0% -> 0%
where the time goes in v1:
time: 43.6 us; the launch traced here: 43.3 us
  Pallas kernels  35.8 us (82%)
  local copies, waits for them, and re-layouts  7.47 us (17%)
    pallas_call x1, Pallas kernels, local(): pl.pallas_call(functools.partial(kernel, n_sub, n_blk, pad), out_shape=ja...  35.8 us
    unnamed x14, local copies, waits for them, and re-layouts  7.47 us

profile of v1, /device:TPU:0, one launch (start us, length us, event | category | flops | bytes accessed | tf_op | source)
XLA Modules:
  0.0 43.3 jit_solution(16911970643766126115)
XLA Ops:
  0.0 0.8 %copy.8.diagonal = bf16[2,128,16]{2,1,0:T(8,128)(2,1)S(1)} copy(bf16[2,128,16]{1,2,0:T(8,128)(2,1)} %param.10) | data formatting | bytes 16384 | tf_op args[2]
  0.8 0.0 copy-start
  0.8 2.2 %copy-done = bf16[2,2048,512]{2,1,0:T(8,128)(2,1)S(1)} copy-done((bf16[2,2048,512]{2,1,0:T(8,128)(2,1)S(1)}, bf16[2,2048,512]{2,1,0:T(8,128)(2,1)}, u32[]{:S(2)}) %copy-start) | copy-done | bytes 4194328
  3.0 0.0 copy-start.1
  3.0 0.9 %copy-done.1 = bf16[2,512,128]{2,1,0:T(8,128)(2,1)S(1)} copy-done((bf16[2,512,128]{2,1,0:T(8,128)(2,1)S(1)}, bf16[2,512,128]{2,1,0:T(8,128)(2,1)}, u32[]{:S(2)}) %copy-start.1) | copy-done | bytes 262168
  4.0 0.0 copy-start.2
  4.0 0.9 %copy-done.2 = bf16[2,16,2048]{2,1,0:T(8,128)(2,1)S(1)} copy-done((bf16[2,16,2048]{2,1,0:T(8,128)(2,1)S(1)}, bf16[2,16,2048]{2,1,0:T(8,128)(2,1)}, u32[]{:S(2)}) %copy-start.2) | copy-done | bytes 131096
  4.9 0.0 copy-start.3
  4.9 0.7 %copy-done.3 = s32[2,128]{1,0:T(2,128)S(1)} copy-done((s32[2,128]{1,0:T(2,128)S(1)}, s32[2,128]{1,0:T(2,128)}, u32[]{:S(2)}) %copy-start.3) | copy-done | bytes 1048
  5.5 0.0 copy-start.4
  5.5 0.7 %copy-done.4 = s32[2,128]{1,0:T(2,128)S(1)} copy-done((s32[2,128]{1,0:T(2,128)S(1)}, s32[2,128]{1,0:T(2,128)}, u32[]{:S(2)}) %copy-start.4) | copy-done | bytes 1048
  6.2 0.0 copy-start.5
  6.2 0.7 %copy-done.5 = s32[2]{0:T(128)S(1)} copy-done((s32[2]{0:T(128)S(1)}, s32[2]{0:T(128)}, u32[]{:S(2)}) %copy-start.5) | copy-done | bytes 32
  6.9 35.8 %shard_map.73 = bf16[2,16,128]{2,1,0:T(8,128)(2,1)S(1)} custom-call(bf16[2,2048,512]{2,1,0:T(8,128)(2,1)S(1)} %copy-done, bf16[2,512,128]{2,1,0:T(8,128)(2,1)S(1)} %copy-done.1, bf16[2,128,16]{2,1,0:T(8,128)(2,1)S(1)} %copy.8.diagonal, bf16[2,16,2048]{2,1,0:T(8,128)(2,1)S(1)} %copy-done.2, s32[2]{0:T(128)S(1)} %copy-done.5, s32[2,128]{1,0:T(2,128)S(1)} %copy-done.3, ...), custom_call_target="tpu_custom_call" | custom-call | flops 1073741824 | bytes 4194304 | tf_op jit(solution)/shard_map/pallas_call | solution.py:244
  42.7 0.6 %copy.10 = bf16[2,16,128]{2,1,0:T(8,128)(2,1)} copy(bf16[2,16,128]{2,1,0:T(8,128)(2,1)S(1)} %shard_map.73) | data formatting | bytes 16384
Async XLA Ops:
  0.8 2.2 %copy-start = (bf16[2,2048,512]{2,1,0:T(8,128)(2,1)S(1)}, bf16[2,2048,512]{2,1,0:T(8,128)(2,1)}, u32[]{:S(2)}) copy-start(bf16[2,2048,512]{2,1,0:T(8,128)(2,1)} %factor.1) | copy-start | bytes 12582916
  3.0 0.9 %copy-start.1 = (bf16[2,512,128]{2,1,0:T(8,128)(2,1)S(1)}, bf16[2,512,128]{2,1,0:T(8,128)(2,1)}, u32[]{:S(2)}) copy-start(bf16[2,512,128]{2,1,0:T(8,128)(2,1)} %samples.1) | copy-start | bytes 786436
  4.0 0.9 %copy-start.2 = (bf16[2,16,2048]{2,1,0:T(8,128)(2,1)S(1)}, bf16[2,16,2048]{2,1,0:T(8,128)(2,1)}, u32[]{:S(2)}) copy-start(bf16[2,16,2048]{2,1,0:T(8,128)(2,1)} %coupling.1) | copy-start | bytes 393220
  4.9 0.7 %copy-start.3 = (s32[2,128]{1,0:T(2,128)S(1)}, s32[2,128]{1,0:T(2,128)}, u32[]{:S(2)}) copy-start(s32[2,128]{1,0:T(2,128)} %peer_device.1) | copy-start | bytes 3076
  5.5 0.7 %copy-start.4 = (s32[2,128]{1,0:T(2,128)S(1)}, s32[2,128]{1,0:T(2,128)}, u32[]{:S(2)}) copy-start(s32[2,128]{1,0:T(2,128)} %peer_lane.1) | copy-start | bytes 3076
  6.2 0.7 %copy-start.5 = (s32[2]{0:T(128)S(1)}, s32[2]{0:T(128)}, u32[]{:S(2)}) copy-start(s32[2]{0:T(128)} %blocks.1) | copy-start | bytes 28

commit v2 on v1

v2 whole, which is shorter than its diff:
```python
import functools

import jax
import jax.numpy as jnp
from jax import lax
from jax.experimental import pallas as pl
from jax.experimental.pallas import tpu as pltpu
from jax.sharding import PartitionSpec as P

FACE_HALF = 104
MESH = pl.DeviceIdType.MESH
F32, BF16 = jnp.float32, jnp.bfloat16


def kernel(
    n_sub, n_blk, pad, main, extra,
    factor, samples, diagonal, coupling, blocks_in, peer_in, lane_in_ref, out,
    fac, drv, tr, parts, near, far, mixed, kept, diag_out, diag_in, main_out, main_in,
    tail_out, tail_in, coup_t, coup_out, coup_in, inner, inner_in, diag_own,
    diag_raw, coup, peer_device, peer_lane, blocks,
    local_sem, small_sem, near_sem, far_sem, relay_sem, near_sum, far_sum, diag_sem, main_sem,
    tail_sem, coup_sem, last_sem,
):
    me, here = lax.axis_index("sub"), lax.axis_index("blk")
    subs, order, quarter = fac.shape
    tile, slots_one = diagonal.shape[1], diagonal.shape[2]
    slots = subs * slots_one
    cols = samples.shape[2]
    mine = tile // n_blk
    inner_rows = coupling.shape[1]
    twin = here + 1 - 2 * lax.rem(here, 2)
    cross = lax.rem(here + 2, n_blk)
    diag = lax.rem(twin + 2, n_blk)

    def remote(src, dst, sems, where):
        return pltpu.make_async_remote_copy(
            src_ref=src, dst_ref=dst, send_sem=sems.at[0], recv_sem=sems.at[1],
            device_id=where, device_id_type=MESH,
        )

    def sub_peer(step):
        return lax.rem(me + step, n_sub)

    barrier = pltpu.get_barrier_semaphore()
    for b in (twin, cross, diag):
        pl.semaphore_signal(barrier, inc=1, device_id={"blk": b}, device_id_type=MESH)

    def greet(step, carry):
        pl.semaphore_signal(
            barrier, inc=1, device_id={"sub": sub_peer(step)}, device_id_type=MESH
        )
        return carry

    lax.fori_loop(1, n_sub, greet, 0)

    small = [
        pltpu.make_async_copy(src, dst, small_sem.at[i])
        for i, (src, dst) in enumerate((
            (blocks_in, blocks), (peer_in, peer_device), (lane_in_ref, peer_lane),
            (diagonal, diag_raw), (coupling, coup),
        ))
    ]
    for c in small:
        c.start()
    own = pltpu.make_async_copy(samples, drv.at[here], local_sem.at[subs])
    own.start()
    load = []
    for s in range(subs):
        one = pltpu.make_async_copy(factor.at[s], fac.at[s], local_sem.at[s])
        one.start()
        load.append(one)

    pl.semaphore_wait(barrier, n_sub - 1 + 3)

    to_far = [
        remote(samples.at[s], drv.at[here, s], far_sem.at[s], {"blk": cross}) for s in range(subs)
    ]
    to_near = [
        remote(samples.at[s], drv.at[here, s], near_sem.at[s], {"blk": twin}) for s in range(subs)
    ]
    for s in range(subs):
        to_far[s].start()
    for s in range(subs):
        to_near[s].start()

    for c in small:
        c.wait()
    slot_of = lax.broadcasted_iota(jnp.int32, (1, slots_one), 1)
    peer_rows, peer_cols, lane_cols = [], [], []
    for s in range(subs):
        peer = jnp.where(slot_of < blocks[s], peer_device[pl.ds(s, 1), :], -1)
        peer_rows.append(peer)
        square = (slots_one, slots_one)
        peer_cols.append(jnp.broadcast_to(peer.astype(F32), square).T[:, :1])
        lanes = peer_lane[pl.ds(s, 1), :].astype(F32)
        lane_cols.append(jnp.broadcast_to(lanes, square).T[:, :1])
    peer_row = jnp.concatenate(peer_rows, axis=1)
    lane_row = jnp.concatenate([peer_lane[pl.ds(s, 1), :] for s in range(subs)], axis=1)
    peer_col = jnp.concatenate(peer_cols, axis=0).astype(jnp.int32)
    lane_col = jnp.concatenate(lane_cols, axis=0).astype(jnp.int32)
    live = peer_col >= 0
    inside = peer_col == me

    def target(peer, lane, size, low, high, offset):
        chosen = (peer >= 0) & (lane >= low) & (lane < high)
        return jnp.where(chosen, peer * size + (lane - low) + offset, -1)

    def place(size, low, high, offset=0):
        row_of = lax.broadcasted_iota(jnp.int32, (n_sub * size, slots), 0)
        wanted = target(peer_row, lane_row, size, low, high, offset)
        return jnp.where(row_of == wanted, 1.0, 0.0).astype(BF16)

    def collect(size, low, high, offset=0):
        lane_of = lax.broadcasted_iota(jnp.int32, (slots, n_sub * size), 1)
        wanted = target(peer_col, lane_col, size, low, high, offset)
        return jnp.where(lane_of == wanted, 1.0, 0.0).astype(BF16)

    def rows_of(index, size):
        return pl.ds(pl.multiple_of(index * size, 16), size)

    def send_faces(value, sent, got, sems, size):
        sent[...] = value.astype(BF16)
        got[rows_of(me, size), :] = sent[rows_of(me, size), :]

        def go(step, carry):
            remote(
                sent.at[rows_of(sub_peer(step), size)], got.at[rows_of(me, size)], sems,
                {"sub": sub_peer(step)},
            ).start()
            return carry

        lax.fori_loop(1, n_sub, go, 0)

    def wait_faces(sent, got, sems, size):
        every = pl.ds(0, (n_sub - 1) * size)
        remote(sent.at[every], got.at[every], sems, {"sub": sub_peer(1)}).wait()

    def dot(left, right):
        return jnp.dot(left, right, preferred_element_type=F32)

    for s in range(subs):
        wide = jnp.concatenate(
            [diag_raw[s].astype(F32), jnp.zeros((cols - tile, slots_one), F32)], axis=0
        )
        diag_own[s * slots_one:(s + 1) * slots_one, :] = wide.T.astype(BF16)
    send_faces(dot(place(pad, 0, pad), diag_own[...]), diag_out, diag_in, diag_sem, pad)

    own.wait()
    row_in = lax.broadcasted_iota(jnp.int32, (quarter, 1), 0)
    lane_in = lax.broadcasted_iota(jnp.int32, (1, quarter), 1)

    def first(s, b):
        begin = pl.multiple_of(b * quarter, quarter)
        rows_live = row_in + begin < blocks[s] * tile
        value = drv[b, s]
        value = jnp.where(rows_live, value, jnp.zeros_like(value))
        return lax.dot_general(
            value, fac[s, pl.ds(begin, quarter), :], (((0,), (0,)), ((), ())),
            preferred_element_type=F32,
        )

    near_copies, far_copies = {}, {}

    def send_near(s):
        span = pl.ds(s * slots_one, slots_one)
        for j, group in ((1, diag), (0, twin)):
            for k in range(mine):
                c = remote(
                    parts.at[group * mine + k, span], near.at[k, j, span],
                    near_sum.at[s, k, j], {"blk": twin},
                )
                c.start()
                near_copies[s, k, j] = c

    def send_far(s):
        span = pl.ds(s * slots_one, slots_one)
        for k in range(mine):
            near_copies[s, k, 1].wait()
            mixed[k, span, :] = (
                parts[cross * mine + k, span, :].astype(F32) + near[k, 1, span, :].astype(F32)
            ).astype(BF16)
            c = remote(mixed.at[k, span], far.at[k, span], far_sum.at[s, k], {"blk": cross})
            c.start()
            far_copies[s, k] = c

    for s in range(subs):
        load[s].wait()
        reduced = first(s, here)
        to_near[s].wait()
        reduced += first(s, twin)
        to_far[s].wait()
        relay = remote(drv.at[cross, s], drv.at[cross, s], relay_sem.at[s], {"blk": twin})
        relay.start()
        reduced += first(s, cross)
        if s:
            send_far(s - 1)
        relay.wait()
        reduced += first(s, diag)
        alive = lane_in + here * quarter < blocks[s] * tile
        reduced = jnp.where(alive, reduced, 0.0).astype(BF16)
        for q in range(0, order, quarter):
            tr[s, q:q + quarter, :] = lax.dot_general(
                fac[s, q:q + quarter, :], reduced, (((1,), (1,)), ((), ())),
                preferred_element_type=F32,
            )
        for t in range(tile):
            parts[t, s * slots_one:(s + 1) * slots_one, :] = tr[
                s, pl.ds(t, slots_one, stride=tile), :
            ].astype(BF16)
        send_near(s)
    send_far(subs - 1)

    tail = None
    for k in range(mine):
        for s in range(subs):
            near_copies[s, k, 0].wait()
            far_copies[s, k].wait()
        kept[k] = (
            parts[here * mine + k].astype(F32) + near[k, 0].astype(F32) + far[k].astype(F32)
        ).astype(BF16)
        if main:
            send_faces(
                dot(place(main, 0, main), kept[k]), main_out.at[k], main_in.at[k], main_sem.at[k],
                main,
            )
        if extra:
            got = dot(place(extra, main, pad, k * (extra // mine)), kept[k])
            tail = got if k == 0 else tail + got
    if extra:
        send_faces(tail, tail_out, tail_in, tail_sem, extra)

    wide = coup[...].reshape(subs * inner_rows, order).astype(F32)
    filler = jnp.zeros((coup_t.shape[1] - subs * inner_rows, order), F32)
    coup_t[...] = jnp.concatenate([wide, filler], axis=0).T
    for t in range(tile):
        piece = coup_t[pl.ds(t, slots_one, stride=tile), :].T
        coup_out[t] = piece[:subs * inner_rows].astype(BF16)
    coup_in[here] = coup_out[pl.ds(here * mine, mine)]
    coup_copies = [
        remote(coup_out.at[pl.ds(b * mine, mine)], coup_in.at[here], coup_sem.at[i], {"blk": b})
        for i, b in enumerate((twin, cross, diag))
    ]
    for c in coup_copies:
        c.start()

    def own_side(value):
        return jnp.where(inside, 0.0, value.astype(F32))

    wait_faces(diag_out, diag_in, diag_sem, pad)
    divisors = own_side(diag_own[...]) + dot(collect(pad, 0, pad), diag_in[...])
    lane_t = lax.broadcasted_iota(jnp.int32, (slots, cols), 1)
    divisor = []
    for k in range(mine):
        one = jnp.sum(jnp.where(lane_t == here * mine + k, divisors, 0.0), axis=1, keepdims=True)
        divisor.append(jnp.where(live, one, 1.0))
    for c in coup_copies:
        c.wait()
    total = []
    for k in range(mine):
        both = own_side(kept[k])
        if main:
            wait_faces(main_out.at[k], main_in.at[k], main_sem.at[k], main)
            both += dot(collect(main, 0, main), main_in[k])
        total.append(both)
    if extra:
        wait_faces(tail_out, tail_in, tail_sem, extra)
        for k in range(mine):
            total[k] += dot(collect(extra, main, pad, k * (extra // mine)), tail_in[...])
    sums = [None] * subs
    for k in range(mine):
        coef = jnp.where(live, total[k] / divisor[k], 0.0).astype(BF16)
        for s in range(subs):
            left = coup_in[:, k, s * inner_rows:(s + 1) * inner_rows, :]
            got = dot(
                left.reshape(n_blk * inner_rows, slots_one),
                coef[s * slots_one:(s + 1) * slots_one],
            )
            sums[s] = got if k == 0 else sums[s] + got
    for s in range(subs):
        inner[:, s] = sums[s].reshape(n_blk, inner_rows, cols)
    last = [
        remote(inner.at[b], inner_in.at[here], last_sem.at[i], {"blk": b})
        for i, b in enumerate((twin, cross, diag))
    ]
    for c in last:
        c.start()
    result = inner[here]
    for c in last:
        c.wait()
    for b in (twin, cross, diag):
        result = result + inner_in[b]
    out[...] = result.astype(BF16)


def local(factor, samples, diagonal, coupling, blocks, peer_device, peer_lane, owns_face):
    n_sub, n_blk = lax.axis_size("sub"), lax.axis_size("blk")
    subs, order, quarter = factor.shape
    slots_one, tile = diagonal.shape[1], diagonal.shape[2]
    slots, cols = subs * slots_one, samples.shape[2]
    mine, inner_rows = tile // n_blk, coupling.shape[1]
    half_cycle = (n_sub - 1) // 2
    capacity = (FACE_HALF + half_cycle - 1) // half_cycle
    pad = -(-capacity // 16) * 16
    main = capacity // 16 * 16
    extra = -(-(capacity - main) * mine // 16) * 16
    flops = 4 * subs * order * quarter * cols
    hbm = pl.BlockSpec(memory_space=pltpu.HBM)
    sem = pltpu.SemaphoreType.DMA
    coup_lanes = -(-subs * inner_rows // 128) * 128

    def vmem(kind, *dims):
        return pltpu.VMEM(tuple(max(d, 1) for d in dims), kind)

    return pl.pallas_call(
        functools.partial(kernel, n_sub, n_blk, pad, main, extra),
        out_shape=jax.ShapeDtypeStruct((subs, inner_rows, cols), BF16),
        in_specs=[hbm] * 7,
        out_specs=pl.BlockSpec(memory_space=pltpu.VMEM),
        scratch_shapes=[
            vmem(BF16, subs, order, quarter),
            vmem(BF16, n_blk, subs, quarter, cols),
            vmem(F32, subs, order, cols),
            vmem(BF16, tile, slots, cols),
            vmem(BF16, mine, 2, slots, cols),
            vmem(BF16, mine, slots, cols),
            vmem(BF16, mine, slots, cols),
            vmem(BF16, mine, slots, cols),
            vmem(BF16, n_sub * pad, cols),
            vmem(BF16, n_sub * pad, cols),
            vmem(BF16, mine, n_sub * main, cols),
            vmem(BF16, mine, n_sub * main, cols),
            vmem(BF16, n_sub * extra, cols),
            vmem(BF16, n_sub * extra, cols),
            vmem(F32, order, coup_lanes),
            vmem(BF16, tile, subs * inner_rows, slots_one),
            vmem(BF16, n_blk, mine, subs * inner_rows, slots_one),
            vmem(F32, n_blk, subs, inner_rows, cols),
            vmem(F32, n_blk, subs, inner_rows, cols),
            vmem(BF16, slots, cols),
            vmem(BF16, subs, tile, slots_one),
            vmem(BF16, *coupling.shape),
            vmem(jnp.int32, *peer_device.shape),
            vmem(jnp.int32, *peer_lane.shape),
            pltpu.SMEM(blocks.shape, jnp.int32),
            sem((subs + 1,)),
            sem((5,)),
            sem((subs, 2)),
            sem((subs, 2)),
            sem((subs, 2)),
            sem((subs, mine, 2, 2)),
            sem((subs, mine, 2)),
            sem((2,)),
            sem((mine, 2)),
            sem((2,)),
            sem((3, 2)),
            sem((3, 2)),
        ],
        compiler_params=pltpu.CompilerParams(
            collective_id=0, has_side_effects=True, vmem_limit_bytes=56 * 1024 * 1024
        ),
        cost_estimate=pl.CostEstimate(
            flops=flops, bytes_accessed=2 * factor.size, transcendentals=0
        ),
    )(factor, samples, jnp.swapaxes(diagonal, 1, 2), coupling, blocks, peer_device, peer_lane)


def solution(mesh):
    placed = (
        P("sub", None, "blk"),
        P("sub", "blk", None),
        P("sub", None, None),
        P("sub", "blk", None),
        P("sub"),
        P("sub", None),
        P("sub", None),
        P("sub", None),
    )
    return jax.shard_map(
        local, mesh=mesh, in_specs=placed, out_specs=P("sub", "blk", None), check_vma=False
    )
```

time: 43.6 us -> 34.8 us (0.80)
  local copies, waits for them, and re-layouts: 7.47 us -> 1.3 us
  Pallas kernels: 35.8 us -> 33.3 us
    unnamed x14 -> x1, local copies, waits for them, and re-layouts: 7.47 us -> 1.3 us
    pallas_call x1, Pallas kernels: 35.8 us -> 33.3 us  [local(): pl.pallas_call(functools.partial(kernel, n_sub, n_blk, pad, main, extra),...]
where the time goes in v2:
time: 34.8 us; the launch traced here: 34.6 us
  Pallas kernels  33.3 us (96%)
  local copies, waits for them, and re-layouts  1.3 us (4%)
    pallas_call x1, Pallas kernels, local(): pl.pallas_call(functools.partial(kernel, n_sub, n_blk, pad, main, extra),...  33.3 us
    unnamed x1, local copies, waits for them, and re-layouts  1.3 us

profile of v2, /device:TPU:0, one launch (start us, length us, event | category | flops | bytes accessed | tf_op | source)
XLA Modules:
  0.0 34.6 jit_solution(16040996413633084310)
XLA Ops:
  0.0 33.3 %shard_map.73 = bf16[2,16,128]{2,1,0:T(8,128)(2,1)} custom-call(bf16[2,2048,512]{2,1,0:T(8,128)(2,1)} %factor.1, bf16[2,512,128]{2,1,0:T(8,128)(2,1)} %samples.1, bf16[2,16,128]{2,1,0:T(8,128)(2,1)} %bitcast.1, bf16[2,16,2048]{2,1,0:T(8,128)(2,1)} %coupling.1, s32[2]{0:T(128)} %blocks_in.1, s32[2,128]{1,0:T(2,128)} %peer_in.1, s32[2,128]{1,0:T(2,128)} %lane_in_ref.1), custom_call_target="tpu_custom_call" | custom-call | flops 1073741824 | bytes 4194304 | tf_op jit(solution)/shard_map/pallas_call | solution.py:314
  33.3 1.3 %copy.9 = bf16[2,16,128]{2,1,0:T(8,128)(2,1)} copy(bf16[2,16,128]{2,1,0:T(8,128)(2,1)} %shard_map.73) | data formatting | bytes 16384

commit v3 on v2

--- a/solution.py
+++ b/solution.py
@@ -41,17 +41,23 @@
     def sub_peer(step):
         return lax.rem(me + step, n_sub)
 
+    def each_peer(act):
+        if n_sub <= 2 * tile:
+            for step in range(1, n_sub):
+                act(step)
+        else:
+            lax.fori_loop(1, n_sub, lambda step, carry: act(step), None)
+
     barrier = pltpu.get_barrier_semaphore()
     for b in (twin, cross, diag):
         pl.semaphore_signal(barrier, inc=1, device_id={"blk": b}, device_id_type=MESH)
 
-    def greet(step, carry):
+    def greet(step):
         pl.semaphore_signal(
             barrier, inc=1, device_id={"sub": sub_peer(step)}, device_id_type=MESH
         )
-        return carry
-
-    lax.fori_loop(1, n_sub, greet, 0)
+
+    each_peer(greet)
 
     small = [
         pltpu.make_async_copy(src, dst, small_sem.at[i])
@@ -122,14 +128,13 @@
         sent[...] = value.astype(BF16)
         got[rows_of(me, size), :] = sent[rows_of(me, size), :]
 
-        def go(step, carry):
+        def go(step):
             remote(
                 sent.at[rows_of(sub_peer(step), size)], got.at[rows_of(me, size)], sems,
                 {"sub": sub_peer(step)},
             ).start()
-            return carry
-
-        lax.fori_loop(1, n_sub, go, 0)
+
+        each_peer(go)
 
     def wait_faces(sent, got, sems, size):
         every = pl.ds(0, (n_sub - 1) * size)
@@ -161,25 +166,33 @@
 
     near_copies, far_copies = {}, {}
 
+    def spans(s):
+        step = 1 if s == subs - 1 else mine
+        return [(k, step) for k in range(0, mine, step)]
+
     def send_near(s):
         span = pl.ds(s * slots_one, slots_one)
         for j, group in ((1, diag), (0, twin)):
-            for k in range(mine):
+            for k, step in spans(s):
                 c = remote(
-                    parts.at[group * mine + k, span], near.at[k, j, span],
-                    near_sum.at[s, k, j], {"blk": twin},
+                    parts.at[pl.ds(group * mine + k, step), span],
+                    near.at[j, pl.ds(k, step), span], near_sum.at[s, k, j], {"blk": twin},
                 )
                 c.start()
                 near_copies[s, k, j] = c
 
     def send_far(s):
         span = pl.ds(s * slots_one, slots_one)
-        for k in range(mine):
+        for k, step in spans(s):
             near_copies[s, k, 1].wait()
-            mixed[k, span, :] = (
-                parts[cross * mine + k, span, :].astype(F32) + near[k, 1, span, :].astype(F32)
+            mixed[k:k + step, span, :] = (
+                parts[pl.ds(cross * mine + k, step), span, :].astype(F32)
+                + near[1, k:k + step, span, :].astype(F32)
             ).astype(BF16)
-            c = remote(mixed.at[k, span], far.at[k, span], far_sum.at[s, k], {"blk": cross})
+            c = remote(
+                mixed.at[k:k + step, span], far.at[k:k + step, span], far_sum.at[s, k],
+                {"blk": cross},
+            )
             c.start()
             far_copies[s, k] = c
 
@@ -213,10 +226,11 @@
     tail = None
     for k in range(mine):
         for s in range(subs):
-            near_copies[s, k, 0].wait()
-            far_copies[s, k].wait()
+            if (s, k) in far_copies:
+                near_copies[s, k, 0].wait()
+                far_copies[s, k].wait()
         kept[k] = (
-            parts[here * mine + k].astype(F32) + near[k, 0].astype(F32) + far[k].astype(F32)
+            parts[here * mine + k].astype(F32) + near[0, k].astype(F32) + far[k].astype(F32)
         ).astype(BF16)
         if main:
             send_faces(
@@ -289,7 +303,7 @@
         c.wait()
     for b in (twin, cross, diag):
         result = result + inner_in[b]
-    out[...] = result.astype(BF16)
+    out[...] = result
 
 
 def local(factor, samples, diagonal, coupling, blocks, peer_device, peer_lane, owns_face):
@@ -313,7 +327,7 @@
 
     return pl.pallas_call(
         functools.partial(kernel, n_sub, n_blk, pad, main, extra),
-        out_shape=jax.ShapeDtypeStruct((subs, inner_rows, cols), BF16),
+        out_shape=jax.ShapeDtypeStruct((subs, inner_rows, cols), F32),
         in_specs=[hbm] * 7,
         out_specs=pl.BlockSpec(memory_space=pltpu.VMEM),
         scratch_shapes=[
@@ -321,7 +335,7 @@
             vmem(BF16, n_blk, subs, quarter, cols),
             vmem(F32, subs, order, cols),
             vmem(BF16, tile, slots, cols),
-            vmem(BF16, mine, 2, slots, cols),
+            vmem(BF16, 2, mine, slots, cols),
             vmem(BF16, mine, slots, cols),
             vmem(BF16, mine, slots, cols),
             vmem(BF16, mine, slots, cols),
@@ -361,7 +375,7 @@
         cost_estimate=pl.CostEstimate(
             flops=flops, bytes_accessed=2 * factor.size, transcendentals=0
         ),
-    )(factor, samples, jnp.swapaxes(diagonal, 1, 2), coupling, blocks, peer_device, peer_lane)
+    )(factor, samples, jnp.swapaxes(diagonal, 1, 2), coupling, blocks, peer_device, peer_lane).astype(BF16)
 
 
 def solution(mesh):

time: 34.8 us -> 35 us (level)
  other arithmetic: 0 us -> 1.32 us
  local copies, waits for them, and re-layouts: 1.3 us -> 0 us
    convert_element_type x0 -> x1, other arithmetic: none -> 1.32 us  [local(): return pl.pallas_call(functools.partial(kernel, n_sub, n_blk, pad, main,...]
    unnamed x1 -> x0, local copies, waits for them, and re-layouts: 1.3 us -> none
where the time goes in v3:
time: 35 us; the launch traced here: 34.8 us
  Pallas kernels  33.5 us (96%)
  other arithmetic  1.32 us (4%)
    pallas_call x1, Pallas kernels, local(): pl.pallas_call(functools.partial(kernel, n_sub, n_blk, pad, main, extra),...  33.5 us
    convert_element_type x1, other arithmetic, local(): return pl.pallas_call(functools.partial(kernel, n_sub, n_blk, pad, main,...  1.32 us

profile of v3, /device:TPU:0, one launch (start us, length us, event | category | flops | bytes accessed | tf_op | source)
XLA Modules:
  0.0 34.8 jit_solution(16530801891734518436)
XLA Ops:
  0.0 33.5 %shard_map.73 = f32[2,16,128]{2,1,0:T(8,128)} custom-call(bf16[2,2048,512]{2,1,0:T(8,128)(2,1)} %factor.1, bf16[2,512,128]{2,1,0:T(8,128)(2,1)} %samples.1, bf16[2,16,128]{2,1,0:T(8,128)(2,1)} %bitcast.1, bf16[2,16,2048]{2,1,0:T(8,128)(2,1)} %coupling.1, s32[2]{0:T(128)} %blocks_in.1, s32[2,128]{1,0:T(2,128)} %peer_in.1, s32[2,128]{1,0:T(2,128)} %lane_in_ref.1), custom_call_target="tpu_custom_call" | custom-call | flops 1073741824 | bytes 4194304 | tf_op jit(solution)/shard_map/pallas_call | solution.py:328
  33.5 1.3 %convert_element_type.3 = bf16[2,16,128]{2,1,0:T(8,128)(2,1)} convert(f32[2,16,128]{2,1,0:T(8,128)} %shard_map.73) | non-fusion elementwise | flops 4096 | bytes 24576 | tf_op jit(solution)/shard_map/convert_element_type | solution.py:378

commit v4 on v3

--- a/solution.py
+++ b/solution.py
@@ -84,8 +84,7 @@
     to_near = [
         remote(samples.at[s], drv.at[here, s], near_sem.at[s], {"blk": twin}) for s in range(subs)
     ]
-    for s in range(subs):
-        to_far[s].start()
+    to_far[0].start()
     for s in range(subs):
         to_near[s].start()
 
@@ -151,6 +150,9 @@
     send_faces(dot(place(pad, 0, pad), diag_own[...]), diag_out, diag_in, diag_sem, pad)
 
     own.wait()
+    for s in range(1, subs):
+        to_far[s - 1].wait_send()
+        to_far[s].start()
     row_in = lax.broadcasted_iota(jnp.int32, (quarter, 1), 0)
     lane_in = lax.broadcasted_iota(jnp.int32, (1, quarter), 1)
 
@@ -181,32 +183,35 @@
                 c.start()
                 near_copies[s, k, j] = c
 
-    def send_far(s):
+    def send_far(s, k, step):
         span = pl.ds(s * slots_one, slots_one)
-        for k, step in spans(s):
-            near_copies[s, k, 1].wait()
-            mixed[k:k + step, span, :] = (
-                parts[pl.ds(cross * mine + k, step), span, :].astype(F32)
-                + near[1, k:k + step, span, :].astype(F32)
-            ).astype(BF16)
-            c = remote(
-                mixed.at[k:k + step, span], far.at[k:k + step, span], far_sum.at[s, k],
-                {"blk": cross},
-            )
-            c.start()
-            far_copies[s, k] = c
+        near_copies[s, k, 1].wait()
+        mixed[k:k + step, span, :] = (
+            parts[pl.ds(cross * mine + k, step), span, :].astype(F32)
+            + near[1, k:k + step, span, :].astype(F32)
+        ).astype(BF16)
+        c = remote(
+            mixed.at[k:k + step, span], far.at[k:k + step, span], far_sum.at[s, k],
+            {"blk": cross},
+        )
+        c.start()
+        far_copies[s, k] = c
 
     for s in range(subs):
         load[s].wait()
         reduced = first(s, here)
         to_near[s].wait()
         reduced += first(s, twin)
-        to_far[s].wait()
+        if s == subs - 1:
+            to_far[s].wait_send()
+        to_far[s].wait_recv()
         relay = remote(drv.at[cross, s], drv.at[cross, s], relay_sem.at[s], {"blk": twin})
         relay.start()
         reduced += first(s, cross)
+        if s > 1:
+            far_copies[s - 2, 0].wait_send()
         if s:
-            send_far(s - 1)
+            send_far(s - 1, 0, mine)
         relay.wait()
         reduced += first(s, diag)
         alive = lane_in + here * quarter < blocks[s] * tile
@@ -221,14 +226,19 @@
                 s, pl.ds(t, slots_one, stride=tile), :
             ].astype(BF16)
         send_near(s)
-    send_far(subs - 1)
+    if subs > 1:
+        far_copies[subs - 2, 0].wait_send()
+    send_far(subs - 1, 0, 1)
 
     tail = None
     for k in range(mine):
+        far_copies[subs - 1, k].wait_send()
+        if k + 1 < mine:
+            send_far(subs - 1, k + 1, 1)
         for s in range(subs):
             if (s, k) in far_copies:
                 near_copies[s, k, 0].wait()
-                far_copies[s, k].wait()
+                far_copies[s, k].wait_recv()
         kept[k] = (
             parts[here * mine + k].astype(F32) + near[0, k].astype(F32) + far[k].astype(F32)
         ).astype(BF16)

time: 35 us -> 37.1 us (1.060)
  Pallas kernels: 33.5 us -> 35.6 us
    pallas_call x1, Pallas kernels: 33.5 us -> 35.6 us  [local(): pl.pallas_call(functools.partial(kernel, n_sub, n_blk, pad, main, extra),...]
where the time goes in v4:
time: 37.1 us; the launch traced here: 36.9 us
  Pallas kernels  35.6 us (96%)
  other arithmetic  1.32 us (4%)
    pallas_call x1, Pallas kernels, local(): pl.pallas_call(functools.partial(kernel, n_sub, n_blk, pad, main, extra),...  35.6 us
    convert_element_type x1, other arithmetic, local(): return pl.pallas_call(functools.partial(kernel, n_sub, n_blk, pad, main,...  1.32 us

profile of v4, /device:TPU:0, one launch (start us, length us, event | category | flops | bytes accessed | tf_op | source)
XLA Modules:
  0.0 36.9 jit_solution(9467778038758199584)
XLA Ops:
  0.0 35.6 %shard_map.73 = f32[2,16,128]{2,1,0:T(8,128)} custom-call(bf16[2,2048,512]{2,1,0:T(8,128)(2,1)} %factor.1, bf16[2,512,128]{2,1,0:T(8,128)(2,1)} %samples.1, bf16[2,16,128]{2,1,0:T(8,128)(2,1)} %bitcast.1, bf16[2,16,2048]{2,1,0:T(8,128)(2,1)} %coupling.1, s32[2]{0:T(128)} %blocks_in.1, s32[2,128]{1,0:T(2,128)} %peer_in.1, s32[2,128]{1,0:T(2,128)} %lane_in_ref.1), custom_call_target="tpu_custom_call" | custom-call | flops 1073741824 | bytes 4194304 | tf_op jit(solution)/shard_map/pallas_call | solution.py:338
  35.6 1.3 %convert_element_type.3 = bf16[2,16,128]{2,1,0:T(8,128)(2,1)} convert(f32[2,16,128]{2,1,0:T(8,128)} %shard_map.73) | non-fusion elementwise | flops 4096 | bytes 24576 | tf_op jit(solution)/shard_map/convert_element_type | solution.py:388

commit v5 on v3

--- a/solution.py
+++ b/solution.py
@@ -170,16 +170,15 @@
         step = 1 if s == subs - 1 else mine
         return [(k, step) for k in range(0, mine, step)]
 
-    def send_near(s):
+    def send_near(s, j, k, step):
         span = pl.ds(s * slots_one, slots_one)
-        for j, group in ((1, diag), (0, twin)):
-            for k, step in spans(s):
-                c = remote(
-                    parts.at[pl.ds(group * mine + k, step), span],
-                    near.at[j, pl.ds(k, step), span], near_sum.at[s, k, j], {"blk": twin},
-                )
-                c.start()
-                near_copies[s, k, j] = c
+        group = diag if j else twin
+        c = remote(
+            parts.at[pl.ds(group * mine + k, step), span],
+            near.at[j, pl.ds(k, step), span], near_sum.at[s, k, j], {"blk": twin},
+        )
+        c.start()
+        near_copies[s, k, j] = c
 
     def send_far(s):
         span = pl.ds(s * slots_one, slots_one)
@@ -216,14 +215,18 @@
                 fac[s, q:q + quarter, :], reduced, (((1,), (1,)), ((), ())),
                 preferred_element_type=F32,
             )
-        for t in range(tile):
-            parts[t, s * slots_one:(s + 1) * slots_one, :] = tr[
-                s, pl.ds(t, slots_one, stride=tile), :
-            ].astype(BF16)
-        send_near(s)
+        for k, step in spans(s):
+            for t in range(tile):
+                if k <= t % mine < k + step:
+                    parts[t, s * slots_one:(s + 1) * slots_one, :] = tr[
+                        s, pl.ds(t, slots_one, stride=tile), :
+                    ].astype(BF16)
+            send_near(s, 1, k, step)
+        for k, step in spans(s):
+            send_near(s, 0, k, step)
     send_far(subs - 1)
 
-    tail = None
+    tail, both_size = None, main + extra
     for k in range(mine):
         for s in range(subs):
             if (s, k) in far_copies:
@@ -232,16 +235,15 @@
         kept[k] = (
             parts[here * mine + k].astype(F32) + near[0, k].astype(F32) + far[k].astype(F32)
         ).astype(BF16)
-        if main:
+        if main and k + 1 < mine:
             send_faces(
                 dot(place(main, 0, main), kept[k]), main_out.at[k], main_in.at[k], main_sem.at[k],
                 main,
             )
-        if extra:
-            got = dot(place(extra, main, pad, k * (extra // mine)), kept[k])
-            tail = got if k == 0 else tail + got
-    if extra:
-        send_faces(tail, tail_out, tail_in, tail_sem, extra)
+        got = dot(place(both_size, main, pad, main + k * (extra // mine)), kept[k])
+        tail = got if k == 0 else tail + got
+    tail += dot(place(both_size, 0, main), kept[mine - 1])
+    send_faces(tail, tail_out, tail_in, tail_sem, both_size)
 
     wide = coup[...].reshape(subs * inner_rows, order).astype(F32)
     filler = jnp.zeros((coup_t.shape[1] - subs * inner_rows, order), F32)
@@ -272,14 +274,14 @@
     total = []
     for k in range(mine):
         both = own_side(kept[k])
-        if main:
+        if main and k + 1 < mine:
             wait_faces(main_out.at[k], main_in.at[k], main_sem.at[k], main)
             both += dot(collect(main, 0, main), main_in[k])
         total.append(both)
-    if extra:
-        wait_faces(tail_out, tail_in, tail_sem, extra)
-        for k in range(mine):
-            total[k] += dot(collect(extra, main, pad, k * (extra // mine)), tail_in[...])
+    wait_faces(tail_out, tail_in, tail_sem, both_size)
+    total[-1] += dot(collect(both_size, 0, main), tail_in[...])
+    for k in range(mine):
+        total[k] += dot(collect(both_size, main, pad, main + k * (extra // mine)), tail_in[...])
     sums = [None] * subs
     for k in range(mine):
         coef = jnp.where(live, total[k] / divisor[k], 0.0).astype(BF16)
@@ -343,8 +345,8 @@
             vmem(BF16, n_sub * pad, cols),
             vmem(BF16, mine, n_sub * main, cols),
             vmem(BF16, mine, n_sub * main, cols),
-            vmem(BF16, n_sub * extra, cols),
-            vmem(BF16, n_sub * extra, cols),
+            vmem(BF16, n_sub * (main + extra), cols),
+            vmem(BF16, n_sub * (main + extra), cols),
             vmem(F32, order, coup_lanes),
             vmem(BF16, tile, subs * inner_rows, slots_one),
             vmem(BF16, n_blk, mine, subs * inner_rows, slots_one),

time: 35 us -> 34.9 us (level)
  no operation moved by 1% of the time
where the time goes in v5:
time: 34.9 us; the launch traced here: 34.7 us
  Pallas kernels  33.3 us (95%)
  other arithmetic  1.32 us (4%)
    pallas_call x1, Pallas kernels, local(): pl.pallas_call(functools.partial(kernel, n_sub, n_blk, pad, main, extra),...  33.3 us
    convert_element_type x1, other arithmetic, local(): return pl.pallas_call(functools.partial(kernel, n_sub, n_blk, pad, main,...  1.32 us

profile of v5, /device:TPU:0, one launch (start us, length us, event | category | flops | bytes accessed | tf_op | source)
XLA Modules:
  0.0 34.7 jit_solution(17892460209447440952)
XLA Ops:
  0.0 33.3 %shard_map.73 = f32[2,16,128]{2,1,0:T(8,128)} custom-call(bf16[2,2048,512]{2,1,0:T(8,128)(2,1)} %factor.1, bf16[2,512,128]{2,1,0:T(8,128)(2,1)} %samples.1, bf16[2,16,128]{2,1,0:T(8,128)(2,1)} %bitcast.1, bf16[2,16,2048]{2,1,0:T(8,128)(2,1)} %coupling.1, s32[2]{0:T(128)} %blocks_in.1, s32[2,128]{1,0:T(2,128)} %peer_in.1, s32[2,128]{1,0:T(2,128)} %lane_in_ref.1), custom_call_target="tpu_custom_call" | custom-call | flops 1073741824 | bytes 4194304 | tf_op jit(solution)/shard_map/pallas_call | solution.py:330
  33.3 1.3 %convert_element_type.3 = bf16[2,16,128]{2,1,0:T(8,128)(2,1)} convert(f32[2,16,128]{2,1,0:T(8,128)} %shard_map.73) | non-fusion elementwise | flops 4096 | bytes 24576 | tf_op jit(solution)/shard_map/convert_element_type | solution.py:380

commit v6 on v5

--- a/solution.py
+++ b/solution.py
@@ -43,7 +43,7 @@
 
     def each_peer(act):
         if n_sub <= 2 * tile:
-            for step in range(1, n_sub):
+            for step in sorted(range(1, n_sub), key=lambda step: abs(2 * step - n_sub)):
                 act(step)
         else:
             lax.fori_loop(1, n_sub, lambda step, carry: act(step), None)
@@ -78,14 +78,22 @@
 
     pl.semaphore_wait(barrier, n_sub - 1 + 3)
 
+    halves = [pl.ds(h * (quarter // 2), quarter // 2) for h in range(2)]
     to_far = [
-        remote(samples.at[s], drv.at[here, s], far_sem.at[s], {"blk": cross}) for s in range(subs)
+        [
+            remote(
+                samples.at[s, half], drv.at[here, s, half], far_sem.at[s, h], {"blk": cross}
+            )
+            for h, half in enumerate(halves)
+        ]
+        for s in range(subs)
     ]
     to_near = [
         remote(samples.at[s], drv.at[here, s], near_sem.at[s], {"blk": twin}) for s in range(subs)
     ]
     for s in range(subs):
-        to_far[s].start()
+        for c in to_far[s]:
+            c.start()
     for s in range(subs):
         to_near[s].start()
 
@@ -200,13 +208,18 @@
         reduced = first(s, here)
         to_near[s].wait()
         reduced += first(s, twin)
-        to_far[s].wait()
-        relay = remote(drv.at[cross, s], drv.at[cross, s], relay_sem.at[s], {"blk": twin})
-        relay.start()
+        relays = []
+        for h, half in enumerate(halves):
+            to_far[s][h].wait()
+            block = drv.at[cross, s, half]
+            relay = remote(block, block, relay_sem.at[s, h], {"blk": twin})
+            relay.start()
+            relays.append(relay)
         reduced += first(s, cross)
         if s:
             send_far(s - 1)
-        relay.wait()
+        for relay in relays:
+            relay.wait()
         reduced += first(s, diag)
         alive = lane_in + here * quarter < blocks[s] * tile
         reduced = jnp.where(alive, reduced, 0.0).astype(BF16)
@@ -361,8 +374,8 @@
             sem((subs + 1,)),
             sem((5,)),
             sem((subs, 2)),
-            sem((subs, 2)),
-            sem((subs, 2)),
+            sem((subs, 2, 2)),
+            sem((subs, 2, 2)),
             sem((subs, mine, 2, 2)),
             sem((subs, mine, 2)),
             sem((2,)),

time: 34.9 us -> 35 us (level)
  no operation moved by 1% of the time
where the time goes in v6:
time: 35 us; the launch traced here: 34.8 us
  Pallas kernels  33.4 us (95%)
  other arithmetic  1.32 us (4%)
    pallas_call x1, Pallas kernels, local(): pl.pallas_call(functools.partial(kernel, n_sub, n_blk, pad, main, extra),...  33.4 us
    convert_element_type x1, other arithmetic, local(): return pl.pallas_call(functools.partial(kernel, n_sub, n_blk, pad, main,...  1.32 us

profile of v6, /device:TPU:0, one launch (start us, length us, event | category | flops | bytes accessed | tf_op | source)
XLA Modules:
  0.0 34.8 jit_solution(3584710719781706413)
XLA Ops:
  0.0 33.4 %shard_map.73 = f32[2,16,128]{2,1,0:T(8,128)} custom-call(bf16[2,2048,512]{2,1,0:T(8,128)(2,1)} %factor.1, bf16[2,512,128]{2,1,0:T(8,128)(2,1)} %samples.1, bf16[2,16,128]{2,1,0:T(8,128)(2,1)} %bitcast.1, bf16[2,16,2048]{2,1,0:T(8,128)(2,1)} %coupling.1, s32[2]{0:T(128)} %blocks_in.1, s32[2,128]{1,0:T(2,128)} %peer_in.1, s32[2,128]{1,0:T(2,128)} %lane_in_ref.1), custom_call_target="tpu_custom_call" | custom-call | flops 1073741824 | bytes 4194304 | tf_op jit(solution)/shard_map/pallas_call | solution.py:343
  33.4 1.3 %convert_element_type.3 = bf16[2,16,128]{2,1,0:T(8,128)(2,1)} convert(f32[2,16,128]{2,1,0:T(8,128)} %shard_map.73) | non-fusion elementwise | flops 4096 | bytes 24576 | tf_op jit(solution)/shard_map/convert_element_type | solution.py:393

commit v7 on v2

--- a/solution.py
+++ b/solution.py
@@ -16,7 +16,7 @@
     n_sub, n_blk, pad, main, extra,
     factor, samples, diagonal, coupling, blocks_in, peer_in, lane_in_ref, out,
     fac, drv, tr, parts, near, far, mixed, kept, diag_out, diag_in, main_out, main_in,
-    tail_out, tail_in, coup_t, coup_out, coup_in, inner, inner_in, diag_own,
+    tail_out, tail_in, coup_t, coup_out, coup_in, inner, diag_own,
     diag_raw, coup, peer_device, peer_lane, blocks,
     local_sem, small_sem, near_sem, far_sem, relay_sem, near_sum, far_sum, diag_sem, main_sem,
     tail_sem, coup_sem, last_sem,
@@ -263,33 +263,37 @@
             both += dot(collect(main, 0, main), main_in[k])
         total.append(both)
     if extra:
+        every = jnp.concatenate(
+            [collect(extra, main, pad, k * (extra // mine)) for k in range(mine)], axis=0
+        )
         wait_faces(tail_out, tail_in, tail_sem, extra)
+        rest = dot(every, tail_in[...])
         for k in range(mine):
-            total[k] += dot(collect(extra, main, pad, k * (extra // mine)), tail_in[...])
-    sums = [None] * subs
-    for k in range(mine):
-        coef = jnp.where(live, total[k] / divisor[k], 0.0).astype(BF16)
-        for s in range(subs):
-            left = coup_in[:, k, s * inner_rows:(s + 1) * inner_rows, :]
-            got = dot(
-                left.reshape(n_blk * inner_rows, slots_one),
-                coef[s * slots_one:(s + 1) * slots_one],
+            total[k] += rest[k * slots:(k + 1) * slots]
+    coefs = [
+        jnp.where(live, total[k] / divisor[k], 0.0).astype(BF16) for k in range(mine)
+    ]
+    for s in range(subs):
+        left = [
+            coup_in[:, k, s * inner_rows:(s + 1) * inner_rows, :].reshape(
+                n_blk * inner_rows, slots_one
             )
-            sums[s] = got if k == 0 else sums[s] + got
-    for s in range(subs):
-        inner[:, s] = sums[s].reshape(n_blk, inner_rows, cols)
+            for k in range(mine)
+        ]
+        right = [coef[s * slots_one:(s + 1) * slots_one] for coef in coefs]
+        got = dot(jnp.concatenate(left, axis=1), jnp.concatenate(right, axis=0))
+        inner[:, s] = got.reshape(n_blk, inner_rows, cols)
     last = [
-        remote(inner.at[b], inner_in.at[here], last_sem.at[i], {"blk": b})
+        remote(inner.at[b], out.at[here], last_sem.at[i], {"blk": b})
         for i, b in enumerate((twin, cross, diag))
     ]
     for c in last:
         c.start()
-    result = inner[here]
+    stay = pltpu.make_async_copy(inner.at[here], out.at[here], local_sem.at[subs])
+    stay.start()
+    stay.wait()
     for c in last:
         c.wait()
-    for b in (twin, cross, diag):
-        result = result + inner_in[b]
-    out[...] = result.astype(BF16)
 
 
 def local(factor, samples, diagonal, coupling, blocks, peer_device, peer_lane, owns_face):
@@ -311,11 +315,11 @@
     def vmem(kind, *dims):
         return pltpu.VMEM(tuple(max(d, 1) for d in dims), kind)
 
-    return pl.pallas_call(
+    shares = pl.pallas_call(
         functools.partial(kernel, n_sub, n_blk, pad, main, extra),
-        out_shape=jax.ShapeDtypeStruct((subs, inner_rows, cols), BF16),
+        out_shape=jax.ShapeDtypeStruct((n_blk, subs, inner_rows, cols), F32),
         in_specs=[hbm] * 7,
-        out_specs=pl.BlockSpec(memory_space=pltpu.VMEM),
+        out_specs=hbm,
         scratch_shapes=[
             vmem(BF16, subs, order, quarter),
             vmem(BF16, n_blk, subs, quarter, cols),
@@ -334,7 +338,6 @@
             vmem(F32, order, coup_lanes),
             vmem(BF16, tile, subs * inner_rows, slots_one),
             vmem(BF16, n_blk, mine, subs * inner_rows, slots_one),
-            vmem(F32, n_blk, subs, inner_rows, cols),
             vmem(F32, n_blk, subs, inner_rows, cols),
             vmem(BF16, slots, cols),
             vmem(BF16, subs, tile, slots_one),
@@ -362,6 +365,7 @@
             flops=flops, bytes_accessed=2 * factor.size, transcendentals=0
         ),
     )(factor, samples, jnp.swapaxes(diagonal, 1, 2), coupling, blocks, peer_device, peer_lane)
+    return jnp.sum(shares, axis=0).astype(BF16)
 
 
 def solution(mesh):

time: 34.8 us -> 34.3 us (0.986)
  other arithmetic: 0 us -> 1.45 us
  local copies, waits for them, and re-layouts: 1.3 us -> 0 us
  Pallas kernels: 33.3 us -> 32.7 us
    reduce_sum x0 -> x1, other arithmetic: none -> 1.45 us  [local(): return jnp.sum(shares, axis=0).astype(BF16)]
    unnamed x1 -> x0, local copies, waits for them, and re-layouts: 1.3 us -> none
    pallas_call x1, Pallas kernels: 33.3 us -> 32.7 us  [local(): pl.pallas_call(functools.partial(kernel, n_sub, n_blk, pad, main, extra),...]
where the time goes in v7:
time: 34.3 us; the launch traced here: 34.2 us
  Pallas kernels  32.7 us (95%)
  other arithmetic  1.45 us (4%)
    pallas_call x1, Pallas kernels, local(): pl.pallas_call(functools.partial(kernel, n_sub, n_blk, pad, main, extra),...  32.7 us
    reduce_sum x1, other arithmetic, local(): return jnp.sum(shares, axis=0).astype(BF16)  1.45 us

profile of v7, /device:TPU:0, one launch (start us, length us, event | category | flops | bytes accessed | tf_op | source)
XLA Modules:
  0.0 34.2 jit_solution(8548280375767747625)
XLA Ops:
  0.0 32.7 %shard_map.73 = f32[4,2,16,128]{3,2,1,0:T(8,128)} custom-call(bf16[2,2048,512]{2,1,0:T(8,128)(2,1)} %factor.1, bf16[2,512,128]{2,1,0:T(8,128)(2,1)} %samples.1, bf16[2,16,128]{2,1,0:T(8,128)(2,1)} %bitcast.1, bf16[2,16,2048]{2,1,0:T(8,128)(2,1)} %coupling.1, s32[2]{0:T(128)} %blocks_in.1, s32[2,128]{1,0:T(2,128)} %peer_in.1, s32[2,128]{1,0:T(2,128)} %lane_in_ref.1), custom_call_target="tpu_custom_call" | custom-call | flops 1073741824 | bytes 4194304 | tf_op jit(solution)/shard_map/pallas_call | solution.py:318
  32.7 1.5 %reduce_sum.9 = bf16[2,16,128]{2,1,0:T(8,128)(2,1)} reduce(f32[4,2,16,128]{3,2,1,0:T(8,128)} %shard_map.73, f32[]{:T(128)} %constant.0.clone.1), dimensions={0}, to_apply=%region_0.0 | reduce | flops 12288 | bytes 73732 | tf_op jit(solution)/shard_map/reduce_sum | solution.py:368

commit v8 on v7

--- a/solution.py
+++ b/solution.py
@@ -42,8 +42,6 @@
         return lax.rem(me + step, n_sub)
 
     barrier = pltpu.get_barrier_semaphore()
-    for b in (twin, cross, diag):
-        pl.semaphore_signal(barrier, inc=1, device_id={"blk": b}, device_id_type=MESH)
 
     def greet(step, carry):
         pl.semaphore_signal(
@@ -52,6 +50,8 @@
         return carry
 
     lax.fori_loop(1, n_sub, greet, 0)
+    for b in (diag, cross, twin):
+        pl.semaphore_signal(barrier, inc=1, device_id={"blk": b}, device_id_type=MESH)
 
     small = [
         pltpu.make_async_copy(src, dst, small_sem.at[i])
@@ -183,17 +183,23 @@
             c.start()
             far_copies[s, k] = c
 
-    for s in range(subs):
+    def begin_sub(s):
         load[s].wait()
-        reduced = first(s, here)
+        held = first(s, here)
         to_near[s].wait()
-        reduced += first(s, twin)
+        return held + first(s, twin)
+
+    later = begin_sub(0)
+    for s in range(subs):
+        reduced = later
         to_far[s].wait()
         relay = remote(drv.at[cross, s], drv.at[cross, s], relay_sem.at[s], {"blk": twin})
         relay.start()
         reduced += first(s, cross)
         if s:
             send_far(s - 1)
+        if s + 1 < subs:
+            later = begin_sub(s + 1)
         relay.wait()
         reduced += first(s, diag)
         alive = lane_in + here * quarter < blocks[s] * tile

time: 34.3 us -> 34.2 us (level)
  no operation moved by 1% of the time
where the time goes in v8:
time: 34.2 us; the launch traced here: 34.1 us
  Pallas kernels  32.6 us (95%)
  other arithmetic  1.45 us (4%)
    pallas_call x1, Pallas kernels, local(): pl.pallas_call(functools.partial(kernel, n_sub, n_blk, pad, main, extra),...  32.6 us
    reduce_sum x1, other arithmetic, local(): return jnp.sum(shares, axis=0).astype(BF16)  1.45 us

profile of v8, /device:TPU:0, one launch (start us, length us, event | category | flops | bytes accessed | tf_op | source)
XLA Modules:
  0.0 34.1 jit_solution(3071108890757604071)
XLA Ops:
  0.0 32.6 %shard_map.73 = f32[4,2,16,128]{3,2,1,0:T(8,128)} custom-call(bf16[2,2048,512]{2,1,0:T(8,128)(2,1)} %factor.1, bf16[2,512,128]{2,1,0:T(8,128)(2,1)} %samples.1, bf16[2,16,128]{2,1,0:T(8,128)(2,1)} %bitcast.1, bf16[2,16,2048]{2,1,0:T(8,128)(2,1)} %coupling.1, s32[2]{0:T(128)} %blocks_in.1, s32[2,128]{1,0:T(2,128)} %peer_in.1, s32[2,128]{1,0:T(2,128)} %lane_in_ref.1), custom_call_target="tpu_custom_call" | custom-call | flops 1073741824 | bytes 4194304 | tf_op jit(solution)/shard_map/pallas_call | solution.py:324
  32.6 1.5 %reduce_sum.9 = bf16[2,16,128]{2,1,0:T(8,128)(2,1)} reduce(f32[4,2,16,128]{3,2,1,0:T(8,128)} %shard_map.73, f32[]{:T(128)} %constant.0.clone.1), dimensions={0}, to_apply=%region_0.0 | reduce | flops 12288 | bytes 73732 | tf_op jit(solution)/shard_map/reduce_sum | solution.py:374

commit v9 on v8

--- a/solution.py
+++ b/solution.py
@@ -190,6 +190,9 @@
         return held + first(s, twin)
 
     later = begin_sub(0)
+    wide = coup[...].reshape(subs * inner_rows, order).astype(F32)
+    filler = jnp.zeros((coup_t.shape[1] - subs * inner_rows, order), F32)
+    coup_t[...] = jnp.concatenate([wide, filler], axis=0).T
     for s in range(subs):
         reduced = later
         to_far[s].wait()
@@ -235,9 +238,6 @@
     if extra:
         send_faces(tail, tail_out, tail_in, tail_sem, extra)
 
-    wide = coup[...].reshape(subs * inner_rows, order).astype(F32)
-    filler = jnp.zeros((coup_t.shape[1] - subs * inner_rows, order), F32)
-    coup_t[...] = jnp.concatenate([wide, filler], axis=0).T
     for t in range(tile):
         piece = coup_t[pl.ds(t, slots_one, stride=tile), :].T
         coup_out[t] = piece[:subs * inner_rows].astype(BF16)
@@ -259,8 +259,6 @@
     for k in range(mine):
         one = jnp.sum(jnp.where(lane_t == here * mine + k, divisors, 0.0), axis=1, keepdims=True)
         divisor.append(jnp.where(live, one, 1.0))
-    for c in coup_copies:
-        c.wait()
     total = []
     for k in range(mine):
         both = own_side(kept[k])
@@ -276,6 +274,8 @@
         rest = dot(every, tail_in[...])
         for k in range(mine):
             total[k] += rest[k * slots:(k + 1) * slots]
+    for c in coup_copies:
+        c.wait()
     coefs = [
         jnp.where(live, total[k] / divisor[k], 0.0).astype(BF16) for k in range(mine)
     ]

time: 34.2 us -> 34.5 us (level)
  no operation moved by 1% of the time
where the time goes in v9:
time: 34.5 us; the launch traced here: 34.3 us
  Pallas kernels  32.9 us (95%)
  other arithmetic  1.45 us (4%)
    pallas_call x1, Pallas kernels, local(): pl.pallas_call(functools.partial(kernel, n_sub, n_blk, pad, main, extra),...  32.9 us
    reduce_sum x1, other arithmetic, local(): return jnp.sum(shares, axis=0).astype(BF16)  1.45 us

profile of v9, /device:TPU:0, one launch (start us, length us, event | category | flops | bytes accessed | tf_op | source)
XLA Modules:
  0.0 34.3 jit_solution(223831386484782046)
XLA Ops:
  0.0 32.9 %shard_map.73 = f32[4,2,16,128]{3,2,1,0:T(8,128)} custom-call(bf16[2,2048,512]{2,1,0:T(8,128)(2,1)} %factor.1, bf16[2,512,128]{2,1,0:T(8,128)(2,1)} %samples.1, bf16[2,16,128]{2,1,0:T(8,128)(2,1)} %bitcast.1, bf16[2,16,2048]{2,1,0:T(8,128)(2,1)} %coupling.1, s32[2]{0:T(128)} %blocks_in.1, s32[2,128]{1,0:T(2,128)} %peer_in.1, s32[2,128]{1,0:T(2,128)} %lane_in_ref.1), custom_call_target="tpu_custom_call" | custom-call | flops 1073741824 | bytes 4194304 | tf_op jit(solution)/shard_map/pallas_call | solution.py:324
  32.9 1.5 %reduce_sum.9 = bf16[2,16,128]{2,1,0:T(8,128)(2,1)} reduce(f32[4,2,16,128]{3,2,1,0:T(8,128)} %shard_map.73, f32[]{:T(128)} %constant.0.clone.1), dimensions={0}, to_apply=%region_0.0 | reduce | flops 12288 | bytes 73732 | tf_op jit(solution)/shard_map/reduce_sum | solution.py:374

commit v10 on v8

--- a/solution.py
+++ b/solution.py
@@ -195,9 +195,9 @@
         to_far[s].wait()
         relay = remote(drv.at[cross, s], drv.at[cross, s], relay_sem.at[s], {"blk": twin})
         relay.start()
-        reduced += first(s, cross)
         if s:
             send_far(s - 1)
+        reduced += first(s, cross)
         if s + 1 < subs:
             later = begin_sub(s + 1)
         relay.wait()
@@ -259,8 +259,6 @@
     for k in range(mine):
         one = jnp.sum(jnp.where(lane_t == here * mine + k, divisors, 0.0), axis=1, keepdims=True)
         divisor.append(jnp.where(live, one, 1.0))
-    for c in coup_copies:
-        c.wait()
     total = []
     for k in range(mine):
         both = own_side(kept[k])
@@ -276,6 +274,8 @@
         rest = dot(every, tail_in[...])
         for k in range(mine):
             total[k] += rest[k * slots:(k + 1) * slots]
+    for c in coup_copies:
+        c.wait()
     coefs = [
         jnp.where(live, total[k] / divisor[k], 0.0).astype(BF16) for k in range(mine)
     ]

time: 34.2 us -> 34.5 us (level)
  no operation moved by 1% of the time
where the time goes in v10:
time: 34.5 us; the launch traced here: 34.3 us
  Pallas kernels  32.9 us (95%)
  other arithmetic  1.45 us (4%)
    pallas_call x1, Pallas kernels, local(): pl.pallas_call(functools.partial(kernel, n_sub, n_blk, pad, main, extra),...  32.9 us
    reduce_sum x1, other arithmetic, local(): return jnp.sum(shares, axis=0).astype(BF16)  1.45 us

profile of v10, /device:TPU:0, one launch (start us, length us, event | category | flops | bytes accessed | tf_op | source)
XLA Modules:
  0.0 34.3 jit_solution(8859877479528726825)
XLA Ops:
  0.0 32.9 %shard_map.73 = f32[4,2,16,128]{3,2,1,0:T(8,128)} custom-call(bf16[2,2048,512]{2,1,0:T(8,128)(2,1)} %factor.1, bf16[2,512,128]{2,1,0:T(8,128)(2,1)} %samples.1, bf16[2,16,128]{2,1,0:T(8,128)(2,1)} %bitcast.1, bf16[2,16,2048]{2,1,0:T(8,128)(2,1)} %coupling.1, s32[2]{0:T(128)} %blocks_in.1, s32[2,128]{1,0:T(2,128)} %peer_in.1, s32[2,128]{1,0:T(2,128)} %lane_in_ref.1), custom_call_target="tpu_custom_call" | custom-call | flops 1073741824 | bytes 4194304 | tf_op jit(solution)/shard_map/pallas_call | solution.py:324
  32.9 1.5 %reduce_sum.9 = bf16[2,16,128]{2,1,0:T(8,128)(2,1)} reduce(f32[4,2,16,128]{3,2,1,0:T(8,128)} %shard_map.73, f32[]{:T(128)} %constant.0.clone.1), dimensions={0}, to_apply=%region_0.0 | reduce | flops 12288 | bytes 73732 | tf_op jit(solution)/shard_map/reduce_sum | solution.py:374
